TPU v7x, 32 devices: a whole 2x2x4 slice. The times are simulated.
32 devices in a mesh: rad: 8 (over z, x), az: 4 (over y, core).
Axes of the slice: x: 2, y: 2, z: 4, core: 2. Of those that a mesh axis runs over, the one named last changes fastest.
Arguments:
- state: float32 [6, 2, 256, 4096], P(None, None, 'rad', 'az'), may hold values from -4 to 4, as said below
- offsets: int32 [256], P('rad'), may hold values from 0 to 4095
- viscosity: float32 [2, 256, 4096], P(None, 'rad', 'az'), may hold values from 0.02 to 0.2
- absorb: float32 [2, 256, 4096], P(None, 'rad', 'az'), may hold values from 0.5 to 8
Outputs:
- new_state: float32 [6, 2, 256, 4096], P(None, None, 'rad', 'az')
- depth: float32 [2, 256, 4096], P(None, 'rad', 'az')
Inputs may be any that keep to these rules, and one draw needn't show every extreme that they name: state[0] lies in 0.5 to 2, state[1], state[2], state[3] in -4 to 4, state[4] in 1 to 3, state[5] in 0.1 to 1.
All inputs are finite; a program needn't handle non-finite values.
Results may differ from a plain program's by a relative error of at most 0.00002.
Values sent between devices are 32-bit elements; how exact they have to be, the bound alone decides.
A program may use at most 128 MiB of HBM per device.

v0:
```python
import functools

import jax
import jax.numpy as jnp
from jax import lax
from jax.experimental import pallas as pl
from jax.experimental.pallas import tpu as pltpu
from jax.sharding import PartitionSpec as P

AZIMUTH_COEF = 0.1
LANES = 128
SUB = 8


def tail_planes(rest):
    cuts = [0, rest // 2, rest]
    return [(a, b - a) for a, b in zip(cuts, cuts[1:]) if b > a]


def kernel(n_rad, n_az, n_local, source, offs, visc_in, absorb_in, result, depth,
           visc, absorb, heat, state, out, buf, sh, eo, ei, tot_out, tot_in, ss, rs, ls):
    groups = n_az // 2
    rad = lax.axis_index("rad")
    az = lax.axis_index("az")
    core = lax.rem(az, 2)
    sibling = {"az": az + 1 - 2 * core}
    planes, rows, width = state.shape
    cols = width // LANES
    tiles = rows // SUB
    dust = planes - 2
    rest = dust
    total_rows = rows * n_rad

    def rad_at(k):
        return {"rad": lax.rem(rad + k + n_rad, n_rad)}

    def az_at(k):
        return {"az": lax.rem(az + 2 * k, n_az)}

    count = [0]

    def remote(src, dst, device):
        i = count[0]
        count[0] += 1
        return pltpu.make_async_remote_copy(
            src_ref=src, dst_ref=dst, send_sem=ss.at[i], recv_sem=rs.at[i],
            device_id=device, device_id_type=pl.DeviceIdType.MESH,
        )

    fetch = pltpu.make_async_copy(source, state, ls.at[0])
    fetches = [fetch] + [
        pltpu.make_async_copy(a, b, ls.at[n_local + i])
        for i, (a, b) in enumerate(((visc_in, visc), (absorb_in, absorb)))
    ]
    stored = []

    def store(p0, np_, r0, nr):
        at = (pl.ds(p0, np_), pl.ds(r0, nr))
        c = pltpu.make_async_copy(out.at[at], result.at[at], ls.at[1 + len(stored)])
        c.start()
        stored.append(c)

    inner, outer = rad > 0, rad < n_rad - 1
    ei[...] = jnp.zeros_like(ei)
    tot_in[...] = jnp.zeros_like(tot_in)
    peers = [az_at(k) for k in range(1, groups)] + [sibling]
    barrier = pltpu.get_barrier_semaphore()
    for there, k in ((inner, -1), (outer, 1)):
        @pl.when(there)
        def _():
            pl.semaphore_signal(barrier, inc=1, device_id=rad_at(k), device_id_type=pl.DeviceIdType.MESH)
    for peer in peers:
        pl.semaphore_signal(barrier, inc=1, device_id=peer, device_id_type=pl.DeviceIdType.MESH)
    senders = len(peers)
    d = 1
    while d < n_rad:
        if d > 1:
            @pl.when(rad >= d)
            def _():
                pl.semaphore_signal(barrier, inc=1, device_id=rad_at(-d), device_id_type=pl.DeviceIdType.MESH)
            senders = senders + (rad + d < n_rad).astype(jnp.int32)
        d *= 2
    pl.semaphore_wait(barrier, senders + inner.astype(jnp.int32) + outer.astype(jnp.int32))

    pieces = [(dust, 2, 0, rows)]
    edge_tiles = [0, tiles - 1]
    for t in edge_tiles + list(range(1, tiles - 2)):
        pieces.append((0, rest, t * SUB, SUB))
    tail = tail_planes(rest)
    for p0, np_ in tail:
        pieces.append((p0, np_, (tiles - 2) * SUB, SUB))

    sent, chained = [], []
    across, beside = [], []
    for p0, np_, r0, nr in pieces:
        ps, rws = pl.ds(p0, np_), pl.ds(r0, nr)
        across.append([remote(source.at[ps, rws], buf.at[2 * k - 1, ps, rws], az_at(k)) for k in range(1, groups)])
        beside.append(remote(source.at[ps, rws], buf.at[0, ps, rws], sibling))
        for c in across[-1]:
            c.start()
            sent.append(c)
    for c in beside:
        c.start()
        sent.append(c)

    def arrive(i):
        p0, np_, r0, nr = pieces[i]
        ps, rws = pl.ds(p0, np_), pl.ds(r0, nr)
        forwards = []
        for k in range(1, groups):
            across[i][k - 1].wait_recv()
            f = remote(buf.at[2 * k - 1, ps, rws], buf.at[2 * k, ps, rws], sibling)
            f.start()
            sent.append(f)
            forwards.append(f)
        beside[i].wait_recv()
        for f in forwards:
            f.wait_recv()

    lane = lax.broadcasted_iota(jnp.int32, (SUB, LANES), 1)

    def shift_tile(tile, p0, np_):
        r = pl.ds(tile * SUB, SUB)
        sub = lax.broadcasted_iota(jnp.int32, (SUB, LANES), 0)
        amount = jnp.full((SUB, LANES), offs[tile * SUB], jnp.int32)
        for k in range(1, SUB):
            amount = jnp.where(sub == k, offs[tile * SUB + k], amount)
        block = amount // width
        within = amount - block * width
        column = within // LANES
        rem = within - column * LANES
        pick = (lane - rem) & (LANES - 1)
        low = lane < rem

        def one(p, carry):
            def load(d, c):
                cs = pl.ds(c * LANES, LANES)
                if d == 0:
                    return state[p, r, cs]
                if d % 2 == 0:
                    return buf[d - 1, p, r, cs]
                slot = jnp.where(core == 1, d, (d + 2) % n_az)
                return buf[slot - 1, p, r, cs]

            line = []
            for move, c in [(1, c) for c in range(cols)] + [(0, c) for c in range(cols)] + [(-1, 0)]:
                value = load(move % n_az, c)
                for b in range(1, n_az):
                    value = jnp.where(block == b, load((b + move) % n_az, c), value)
                line.append(value)
            step = cols // 2
            while step:
                chosen = (column & step) != 0
                line = [jnp.where(chosen, line[i - step], line[i]) for i in range(step, len(line))]
                step //= 2
            turned = [jnp.take_along_axis(v, pick, axis=1, mode="promise_in_bounds") for v in line]
            x = [turned[0]] + [jnp.where(low, turned[j - 1], turned[j]) for j in range(1, len(turned))]
            right = [pltpu.roll(v, 1, 1) for v in x[:-1]]
            left = [pltpu.roll(v, LANES - 1, 1) for v in x[1:]]
            for c in range(cols):
                cs = pl.ds(c * LANES, LANES)
                mid = x[c + 1]
                prev = jnp.where(lane == 0, right[c], right[c + 1])
                nxt = jnp.where(lane == LANES - 1, left[c + 1], left[c])
                sh[p, pl.ds(SUB + tile * SUB, SUB), cs] = mid
                out[p, r, cs] = mid + AZIMUTH_COEF * (nxt + prev - 2.0 * mid)
                if tile == 0:
                    eo[0, p, :, cs] = mid[:1]
                if tile == tiles - 1:
                    eo[1, p, :, cs] = mid[SUB - 1:]
            return carry

        lax.fori_loop(p0, p0 + np_, one, 0)

    hops = []

    def scan_send():
        i = len(hops)
        d = 1 << i
        if d < n_rad:
            c = remote(tot_out.at[i], tot_in.at[i], rad_at(d))
            goes = rad + d < n_rad
            pl.when(goes)(c.start)
            chained.append((goes, c))
            hops.append(c)

    def scan_take():
        i = len(hops) - 1
        pl.when(rad >= 1 << i)(hops[i].wait_recv)
        tot_out[i + 1] = tot_out[i] + tot_in[i]

    def send_edge(side, p0, np_):
        ps = pl.ds(p0, np_)
        c = remote(eo.at[side, ps], ei.at[1 - side, ps], rad_at(-1 if side == 0 else 1))
        goes, comes = (inner, outer) if side == 0 else (outer, inner)
        pl.when(goes)(c.start)
        chained.append((goes, c))
        return comes, c

    def edge_wait(edge):
        pl.when(edge[0])(edge[1].wait_recv)

    def place_edges(p0, np_):
        def one(p, carry):
            sh[p, SUB - 1:SUB, :] = jnp.where(rad > 0, ei[0, p], 0.0)
            sh[p, SUB + rows:SUB + rows + 1, :] = jnp.where(rad < n_rad - 1, ei[1, p], 0.0)
            return carry

        lax.fori_loop(p0, p0 + np_, one, 0)

    def smooth(tile, p0, np_):
        top = SUB + tile * SUB

        def one(p, carry):
            r = pl.ds(tile * SUB, SUB)
            mid = sh[p, top:top + SUB, :]
            up = sh[p, top - 1:top + SUB - 1, :]
            down = sh[p, top + 1:top + SUB + 1, :]
            out[p, r, :] = out[p, r, :] + visc[lax.rem(p, 2), r, :] * (down + up - 2.0 * mid)
            return carry

        lax.fori_loop(p0, p0 + np_, one, 0)

    for c in fetches:
        c.start()
    arrive(0)
    for c in fetches:
        c.wait()
    for t in range(tiles):
        shift_tile(t, dust, 2)
    edges = [send_edge(s, dust, 2) for s in (0, 1)]
    for e in edges:
        edge_wait(e)
    place_edges(dust, 2)
    for t in range(tiles):
        smooth(t, dust, 2)
    store(dust, 2, 0, rows)

    row = lax.broadcasted_iota(jnp.int32, (SUB, width), 0)
    for h in range(2):
        base = jnp.zeros((1, width), jnp.float32)
        for t in range(tiles):
            r = pl.ds(t * SUB, SUB)
            step = 2.0 * absorb[h, r, :] * out[dust + h, r, :] / total_rows
            run = step
            for k in (1, 2, 4):
                run = run + jnp.where(row >= k, pltpu.roll(run, k, 0), 0.0)
            run = run + base
            depth[h, r, :] = run - 0.5 * step
            base = run[SUB - 1:]
        tot_out[0, h] = base
    scan_send()
    arrive(1)
    shift_tile(0, 0, rest)
    edge_in = send_edge(0, 0, rest)
    scan_take()
    scan_send()
    arrive(2)
    shift_tile(tiles - 1, 0, rest)
    edge_out = send_edge(1, 0, rest)

    scan_take()
    while 1 << len(hops) < n_rad:
        scan_send()
        scan_take()
    for h in range(2):
        carried = tot_in[0, h]
        for i in range(1, len(hops)):
            carried = carried + tot_in[i, h]
        for t in range(tiles):
            r = pl.ds(t * SUB, SUB)
            radius = (rad * rows + t * SUB + row).astype(jnp.float32) + 0.5
            flux = 1.0 / (1.0 + radius / total_rows)
            depth[h, r, :] = depth[h, r, :] + carried
            heat[h, r, :] = flux * jnp.exp(-depth[h, r, :])

    def warm(tile):
        r = pl.ds(tile * SUB, SUB)
        for h in range(2):
            out[rest - 2 + h, r, :] = out[rest - 2 + h, r, :] + heat[h, r, :]

    edge_wait(edge_in)
    edge_wait(edge_out)
    place_edges(0, rest)
    i = 3
    for t in range(1, tiles - 2):
        arrive(i)
        shift_tile(t, 0, rest)
        smooth(t - 1, 0, rest)
        warm(t - 1)
        store(0, rest, (t - 1) * SUB, SUB)
        i += 1
    first = max(tiles - 3, 0)
    for p0, np_ in tail:
        arrive(i)
        shift_tile(tiles - 2, p0, np_)
        for t in range(first, tiles):
            smooth(t, p0, np_)
            if p0 + np_ == rest:
                warm(t)
        store(p0, np_, first * SUB, (tiles - first) * SUB)
        i += 1
    for c in stored:
        c.wait()
    for goes, c in chained:
        pl.when(goes)(c.wait_send)
    for c in sent:
        c.wait_send()


def body(n_rad, n_az, state, offsets, viscosity, absorb):
    fields, polar, rows, width = state.shape
    planes = fields * polar
    groups = n_az // 2
    tiles = rows // SUB
    n_tail = len(tail_planes(planes - 2))
    n_pieces = 1 + 2 + max(tiles - 3, 0) + n_tail
    n_scan = (n_rad - 1).bit_length()
    n_local = 2 + max(tiles - 3, 0) + n_tail
    n_sems = n_pieces * (2 * (groups - 1) + 1) + 4 + n_scan
    f32 = jnp.float32
    vm = pl.BlockSpec(memory_space=pltpu.VMEM)
    hbm = pl.BlockSpec(memory_space=pl.ANY)
    moved, local = pl.pallas_call(
        functools.partial(kernel, n_rad, n_az, n_local),
        out_shape=(
            jax.ShapeDtypeStruct((planes, rows, width), f32),
            jax.ShapeDtypeStruct((polar, rows, width), f32),
        ),
        in_specs=[hbm, pl.BlockSpec(memory_space=pltpu.SMEM), hbm, hbm],
        out_specs=(hbm, vm),
        scratch_shapes=[
            pltpu.VMEM((polar, rows, width), f32),
            pltpu.VMEM((polar, rows, width), f32),
            pltpu.VMEM((polar, rows, width), f32),
            pltpu.VMEM((planes, rows, width), f32),
            pltpu.VMEM((planes, rows, width), f32),
            pltpu.VMEM((n_az - 1, planes, rows, width), f32),
            pltpu.VMEM((planes, rows + 2 * SUB, width), f32),
            pltpu.VMEM((2, planes, 1, width), f32),
            pltpu.VMEM((2, planes, 1, width), f32),
            pltpu.VMEM((n_scan + 1, polar, 1, width), f32),
            pltpu.VMEM((n_scan, polar, 1, width), f32),
            pltpu.SemaphoreType.DMA((n_sems,)),
            pltpu.SemaphoreType.DMA((n_sems,)),
            pltpu.SemaphoreType.DMA((n_local + 2,)),
        ],
        compiler_params=pltpu.CompilerParams(
            collective_id=0, has_side_effects=True, vmem_limit_bytes=56 * 2**20
        ),
    )(state.reshape(planes, rows, width), offsets, viscosity, absorb)
    moved = moved.reshape(state.shape)
    return moved, local


def solution(mesh):
    in_specs = (P(None, None, "rad", "az"), P("rad"), P(None, "rad", "az"), P(None, "rad", "az"))
    out_specs = (P(None, None, "rad", "az"), P(None, "rad", "az"))
    f = functools.partial(body, mesh.shape["rad"], mesh.shape["az"])
    return jax.shard_map(f, mesh=mesh, in_specs=in_specs, out_specs=out_specs, check_vma=False)
```

profile of v0, /device:TPU:0, one launch (start us, length us, event | category | flops | bytes accessed | tf_op | source)
XLA Modules:
  0.0 49.1 jit_solution(13905562408317678621)
XLA Ops:
  0.6 45.0 %shard_map.59 = (f32[12,32,1024]{2,1,0:T(8,128)}, f32[2,32,1024]{2,1,0:T(8,128)}) custom-call(f32[12,32,1024]{2,1,0:T(8,128)} %bitcast.2, s32[32]{0:T(128)} %offs.1, f32[2,32,1024]{2,1,0:T(8,128)} %visc_in.1, f32[2,32,1024]{2,1,0:T(8,128)} %absorb_in.1), custom_call_target="tpu_custom_call" | custom-call | tf_op jit(solution)/shard_map/pallas_call | solution.py:324
  45.6 0.0 copy-start
  45.6 2.8 %copy.8 = f32[6,2,32,1024]{3,2,1,0:T(8,128)} copy(f32[6,2,32,1024]{3,2,1,0:T(8,128)} %bitcast.3) | data formatting | bytes 3145728
  48.4 0.0 copy-done
  48.4 0.7 %copy.9 = f32[2,32,1024]{2,1,0:T(8,128)} copy(f32[2,32,1024]{2,1,0:T(8,128)S(1)} %copy-done) | data formatting | bytes 524288
Async XLA Ops:
  45.6 2.8 %copy-start = (f32[2,32,1024]{2,1,0:T(8,128)S(1)}, f32[2,32,1024]{2,1,0:T(8,128)}, u32[]{:S(2)}) copy-start(f32[2,32,1024]{2,1,0:T(8,128)} %get-tuple-element.9) | copy-start | bytes 786436
where the time goes:
time: 49.3 us; the launch traced here: 49.1 us
  Pallas kernels  45 us (91%)
  local copies, waits for them, and re-layouts  3.48 us (7%)
  between operations  0.65 us (1%)
    pallas_call x1, Pallas kernels, body(): pl.pallas_call(functools.partial(kernel, n_rad, n_az, n_local), out_shape...  45 us
    unnamed x4, local copies, waits for them, and re-layouts  3.48 us

commit v1 on v0

--- a/solution.py
+++ b/solution.py
@@ -17,8 +17,8 @@
     return [(a, b - a) for a, b in zip(cuts, cuts[1:]) if b > a]
 
 
-def kernel(n_rad, n_az, n_local, source, offs, visc_in, absorb_in, result, depth,
-           visc, absorb, heat, state, out, buf, sh, eo, ei, tot_out, tot_in, ss, rs, ls):
+def kernel(n_rad, n_az, n_local, source, offs, visc_in, absorb_in, out, depth,
+           visc, absorb, heat, state, buf, sh, eo, ei, tot_out, tot_in, ss, rs, ls):
     groups = n_az // 2
     rad = lax.axis_index("rad")
     az = lax.axis_index("az")
@@ -52,14 +52,6 @@
         pltpu.make_async_copy(a, b, ls.at[n_local + i])
         for i, (a, b) in enumerate(((visc_in, visc), (absorb_in, absorb)))
     ]
-    stored = []
-
-    def store(p0, np_, r0, nr):
-        at = (pl.ds(p0, np_), pl.ds(r0, nr))
-        c = pltpu.make_async_copy(out.at[at], result.at[at], ls.at[1 + len(stored)])
-        c.start()
-        stored.append(c)
-
     inner, outer = rad > 0, rad < n_rad - 1
     ei[...] = jnp.zeros_like(ei)
     tot_in[...] = jnp.zeros_like(tot_in)
@@ -234,7 +226,6 @@
     place_edges(dust, 2)
     for t in range(tiles):
         smooth(t, dust, 2)
-    store(dust, 2, 0, rows)
 
     row = lax.broadcasted_iota(jnp.int32, (SUB, width), 0)
     for h in range(2):
@@ -288,7 +279,6 @@
         shift_tile(t, 0, rest)
         smooth(t - 1, 0, rest)
         warm(t - 1)
-        store(0, rest, (t - 1) * SUB, SUB)
         i += 1
     first = max(tiles - 3, 0)
     for p0, np_ in tail:
@@ -298,10 +288,7 @@
             smooth(t, p0, np_)
             if p0 + np_ == rest:
                 warm(t)
-        store(p0, np_, first * SUB, (tiles - first) * SUB)
         i += 1
-    for c in stored:
-        c.wait()
     for goes, c in chained:
         pl.when(goes)(c.wait_send)
     for c in sent:
@@ -316,7 +303,7 @@
     n_tail = len(tail_planes(planes - 2))
     n_pieces = 1 + 2 + max(tiles - 3, 0) + n_tail
     n_scan = (n_rad - 1).bit_length()
-    n_local = 2 + max(tiles - 3, 0) + n_tail
+    n_local = 1
     n_sems = n_pieces * (2 * (groups - 1) + 1) + 4 + n_scan
     f32 = jnp.float32
     vm = pl.BlockSpec(memory_space=pltpu.VMEM)
@@ -324,16 +311,15 @@
     moved, local = pl.pallas_call(
         functools.partial(kernel, n_rad, n_az, n_local),
         out_shape=(
-            jax.ShapeDtypeStruct((planes, rows, width), f32),
-            jax.ShapeDtypeStruct((polar, rows, width), f32),
+            pltpu.VMEM((planes, rows, width), f32),
+            pltpu.VMEM((polar, rows, width), f32),
         ),
         in_specs=[hbm, pl.BlockSpec(memory_space=pltpu.SMEM), hbm, hbm],
-        out_specs=(hbm, vm),
+        out_specs=(vm, vm),
         scratch_shapes=[
             pltpu.VMEM((polar, rows, width), f32),
             pltpu.VMEM((polar, rows, width), f32),
             pltpu.VMEM((polar, rows, width), f32),
-            pltpu.VMEM((planes, rows, width), f32),
             pltpu.VMEM((planes, rows, width), f32),
             pltpu.VMEM((n_az - 1, planes, rows, width), f32),
             pltpu.VMEM((planes, rows + 2 * SUB, width), f32),

time: 49.3 us -> 46.1 us (0.935)
  local copies, waits for them, and re-layouts: 3.48 us -> 1.85 us
  Pallas kernels: 45 us -> 43.5 us
    unnamed x4 -> x2, local copies, waits for them, and re-layouts: 3.48 us -> 1.85 us
    pallas_call x1, Pallas kernels: 45 us -> 43.5 us  [body(): pl.pallas_call(functools.partial(kernel, n_rad, n_az, n_local), out_shape...]
where the time goes in v1:
time: 46.1 us; the launch traced here: 46 us
  Pallas kernels  43.5 us (94%)
  local copies, waits for them, and re-layouts  1.85 us (4%)
  between operations  0.64 us (1%)
    pallas_call x1, Pallas kernels, body(): pl.pallas_call(functools.partial(kernel, n_rad, n_az, n_local), out_shape...  43.5 us
    unnamed x2, local copies, waits for them, and re-layouts  1.85 us

profile of v1, /device:TPU:0, one launch (start us, length us, event | category | flops | bytes accessed | tf_op | source)
XLA Modules:
  0.0 46.0 jit_solution(16459235949282813111)
XLA Ops:
  0.6 43.5 %shard_map.59 = (f32[12,32,1024]{2,1,0:T(8,128)S(1)}, f32[2,32,1024]{2,1,0:T(8,128)S(1)}) custom-call(f32[12,32,1024]{2,1,0:T(8,128)} %bitcast.3, s32[32]{0:T(128)} %offs.1, f32[2,32,1024]{2,1,0:T(8,128)} %visc_in.1, f32[2,32,1024]{2,1,0:T(8,128)} %absorb_in.1), custom_call_target="tpu_custom_call" | custom-call | tf_op jit(solution)/shard_map/pallas_call | solution.py:311
  44.1 1.1 %copy.8 = f32[6,2,32,1024]{3,2,1,0:T(8,128)} copy(f32[6,2,32,1024]{3,2,1,0:T(8,128)S(1)} %bitcast.2) | data formatting | bytes 3145728
  45.3 0.7 %copy.9 = f32[2,32,1024]{2,1,0:T(8,128)} copy(f32[2,32,1024]{2,1,0:T(8,128)S(1)} %get-tuple-element.7) | data formatting | bytes 524288

commit v2 on v1

--- a/solution.py
+++ b/solution.py
@@ -10,6 +10,8 @@
 AZIMUTH_COEF = 0.1
 LANES = 128
 SUB = 8
+LANE_BITS = 7
+SUB_BITS = 3
 
 
 def tail_planes(rest):
@@ -295,7 +297,7 @@
         c.wait_send()
 
 
-def body(n_rad, n_az, state, offsets, viscosity, absorb):
+def full(n_rad, n_az, state, offsets, viscosity, absorb):
     fields, polar, rows, width = state.shape
     planes = fields * polar
     groups = n_az // 2
@@ -335,8 +337,479 @@
             collective_id=0, has_side_effects=True, vmem_limit_bytes=56 * 2**20
         ),
     )(state.reshape(planes, rows, width), offsets, viscosity, absorb)
-    moved = moved.reshape(state.shape)
     return moved, local
+
+
+def fast_kernel(n_rad, n_az, cap, source, offs, visc_in, absorb_in, out, depth, flag,
+                visc, absorb, heat, gathered, packed, pool_mine, pool_other, early_mine, early_other,
+                stage, sh, eo, ei, tot_out, tot_in, take_v, look_v, take, look, ss, rs, ls):
+    rad = lax.axis_index("rad")
+    az = lax.axis_index("az")
+    core = lax.rem(az, 2)
+    chip = az // 2
+    sibling = {"az": az + 1 - 2 * core}
+    across = {"az": lax.rem(az + 2, n_az)}
+    planes, rows, width = out.shape
+    polar = 2
+    fields = planes // polar
+    cols = width // LANES
+    col_bits = cols.bit_length() - 1
+    tiles = rows // SUB
+    units = rows * cols
+    half = 2 * units
+    ring = 2 * cols
+    span = cols + 2
+    total_rows = rows * n_rad
+    dust, energy = fields - 1, fields - 2
+    order = [dust, energy] + list(range(energy))
+    last = order[-1]
+    n_scan = (n_rad - 1).bit_length()
+    n_early = 2 * ring
+
+    def rad_at(k):
+        return {"rad": lax.rem(rad + k + n_rad, n_rad)}
+
+    def rad_pair(i):
+        d = 1 << i
+        upper = lax.rem(rad // d, 2)
+        return {"rad": rad + d - 2 * d * upper}, upper
+
+    count = [0, 0]
+
+    def remote(src, dst, device):
+        i = count[0]
+        count[0] += 1
+        return pltpu.make_async_remote_copy(
+            src_ref=src, dst_ref=dst, send_sem=ss.at[i], recv_sem=rs.at[i],
+            device_id=device, device_id_type=pl.DeviceIdType.MESH,
+        )
+
+    def local(src, dst):
+        i = count[1]
+        count[1] += 1
+        c = pltpu.make_async_copy(src, dst, ls.at[i])
+        c.start()
+        return c
+
+    inner, outer = rad > 0, rad < n_rad - 1
+    ei[...] = jnp.zeros_like(ei)
+    barrier = pltpu.get_barrier_semaphore()
+    for peer in [sibling, across] + [rad_pair(i)[0] for i in range(1, n_scan)]:
+        pl.semaphore_signal(barrier, inc=1, device_id=peer, device_id_type=pl.DeviceIdType.MESH)
+    for there, k in ((inner, -1), (outer, 1)):
+        @pl.when(there)
+        def _():
+            pl.semaphore_signal(barrier, inc=1, device_id=rad_at(k), device_id_type=pl.DeviceIdType.MESH)
+
+    mine = pl.ds(core * units, units)
+    first_pack = [local(source.at[polar * f + core], gathered[f].at[mine]) for f in order[:2]]
+
+    pl.semaphore_wait(barrier, 2 + n_scan - 1 + inner.astype(jnp.int32) + outer.astype(jnp.int32))
+
+    sent, chained = [], []
+    to_pack = [remote(source.at[polar * f + 1 - core], gathered[f].at[mine], sibling) for f in order]
+    to_mine = [remote(source.at[polar * f + 1 - core], pool_mine[f].at[mine], sibling) for f in order]
+    to_other = [remote(source.at[polar * f + core], pool_other[f].at[mine], sibling) for f in order]
+    to_early = [
+        remote(source.at[polar * last + 1 - core], early_mine.at[mine], sibling),
+        remote(source.at[polar * last + core], early_other.at[mine], sibling),
+    ]
+    sent += to_pack + to_mine + to_other + to_early
+    for c in to_pack[:2]:
+        c.start()
+    own_pack = first_pack + [local(source.at[polar * f + core], gathered[f].at[mine]) for f in order[2:]]
+    own_mine = [local(source.at[polar * f + core], pool_mine[f].at[mine]) for f in order]
+    own_other = [local(source.at[polar * f + 1 - core], pool_other[f].at[mine]) for f in order]
+    own_early = [
+        local(source.at[polar * last + core], early_mine.at[mine]),
+        local(source.at[polar * last + 1 - core], early_other.at[mine]),
+    ]
+    params = [local(visc_in, visc), local(absorb_in, absorb)]
+
+    lane = lax.broadcasted_iota(jnp.int32, (SUB, LANES), 1)
+    sub = lax.broadcasted_iota(jnp.int32, (SUB, LANES), 0)
+
+    def row_offsets(numbers):
+        amount = jnp.full((SUB, LANES), offs[numbers[0]], jnp.int32)
+        for k in range(1, len(numbers)):
+            amount = jnp.where(sub == k, offs[numbers[k]], amount)
+        return amount
+
+    def block_unit(b):
+        return (b >> col_bits) * units + (b & (cols - 1)) * SUB
+
+    shifts = [row_offsets([t * SUB + k for k in range(SUB)]) for t in range(tiles)]
+    leads, manys, befores = [], [], []
+    used = jnp.zeros((SUB, LANES), jnp.int32)
+    for off in shifts:
+        lead = jnp.where(off == 0, ring - 1, jnp.where(off < 2 * width, (2 * width - 1 - off) >> LANE_BITS, 0))
+        many = jnp.where(off < 2 * width, ring - lead, jnp.minimum(((4 * width - off) >> LANE_BITS) + 1, ring))
+        many = jnp.where(off == 0, 2, many)
+        run = many
+        for k in (1, 2, 4):
+            run = run + jnp.where(sub >= k, pltpu.roll(run, k, 0), 0)
+        leads.append(lead)
+        manys.append(many)
+        befores.append(run - many + used)
+        used = used + jnp.broadcast_to(run[SUB - 1:], (SUB, LANES))
+    top_many = jnp.broadcast_to(manys[0][:1], (SUB, LANES))
+    bottom_many = jnp.broadcast_to(manys[-1][SUB - 1:], (SUB, LANES))
+    bases = []
+    for t in range(tiles):
+        base = befores[t] + bottom_many
+        if t == 0:
+            base = jnp.where(sub == 0, 0, base)
+        if t == tiles - 1:
+            base = jnp.where(sub == SUB - 1, top_many, base)
+        bases.append(base)
+    for q in range(-(-cap // LANES)):
+        j = q * LANES + lane
+        place = jnp.zeros((SUB, LANES), jnp.int32)
+        ahead = jnp.zeros((SUB, LANES), jnp.int32)
+        for t in range(tiles):
+            held = (j >= bases[t]) & (j < bases[t] + manys[t])
+            place = place + jnp.where(held, t * SUB * cols + sub, 0)
+            ahead = ahead + jnp.where(held, leads[t] - bases[t], 0)
+        for k in (4, 2, 1):
+            place = place + pltpu.roll(place, k, 0)
+            ahead = ahead + pltpu.roll(ahead, k, 0)
+        take_v[q:q + 1, :] = (block_unit((j + ahead) & (ring - 1)) + place)[:1]
+    take_copy = local(take_v, take)
+    for t in range(tiles):
+        b = az * cols - (shifts[t] >> LANE_BITS) - 1 + lane + 2 * ring
+        near = block_unit(b & (ring - 1)) + (t * SUB * cols + sub)
+        far = half + jnp.minimum(bases[t] + ((b - leads[t]) & (ring - 1)), cap - 1)
+        look_v[t * SUB:(t + 1) * SUB, :] = jnp.where(((b >> (col_bits + 1)) & 1) == chip, near, far)
+    look_copy = local(look_v, look)
+
+    crossing = {f: [] for f in order}
+    cuts = {f: [0, cap // 2 // SUB * SUB, cap] for f in order}
+    cuts[last] = [n_early, (n_early + cap) // 2 // SUB * SUB, cap]
+
+    def pack(some, lo, hi):
+        def eight(k, carry):
+            for s in range(SUB):
+                u = take[k >> 4, (k & 15) * SUB + s]
+                for f in some:
+                    packed[f][pl.ds(k * SUB + s, 1), :] = gathered[f][pl.ds(u, 1), :]
+            return carry
+
+        lax.fori_loop(lo // SUB, hi // SUB, eight, 0)
+
+    def pack_ready(f):
+        own_pack[order.index(f)].wait()
+        to_pack[order.index(f)].wait_recv()
+
+    def pack_send(f):
+        for lo, hi in zip(cuts[f], cuts[f][1:]):
+            pack([f], lo, hi)
+            c = remote(packed[f].at[pl.ds(lo, hi - lo)], pool_mine[f].at[pl.ds(half + lo, hi - lo)], across)
+            c.start()
+            sent.append(c)
+            crossing[f].append(c)
+
+    def shift_rows(numbers, shift, source_ref, slot, write):
+        for s, r in enumerate(numbers):
+            for i in range(span):
+                u = look[r, i]
+                stage[slot, i, s:s + 1, :] = source_ref[pl.ds(u, 1), :]
+        rem = shift & (LANES - 1)
+        pick = (lane - rem) & (LANES - 1)
+        low = lane < rem
+        turned = [
+            jnp.take_along_axis(stage[slot, i], pick, axis=1, mode="promise_in_bounds") for i in range(span)
+        ]
+        x = [turned[0]] + [jnp.where(low, turned[j - 1], turned[j]) for j in range(1, span)]
+        write(x)
+
+    def shift_plane(f, source_ref, p):
+        def one(tile, slot):
+            r = pl.ds(pl.multiple_of(tile * SUB, SUB), SUB)
+            below = pl.ds(pl.multiple_of(SUB + tile * SUB, SUB), SUB)
+
+            def write(x):
+                right = [pltpu.roll(v, 1, 1) for v in x[:-1]]
+                left = [pltpu.roll(v, LANES - 1, 1) for v in x[1:]]
+                for c in range(cols):
+                    cs = pl.ds(c * LANES, LANES)
+                    mid = x[c + 1]
+                    prev = jnp.where(lane == 0, right[c], right[c + 1])
+                    nxt = jnp.where(lane == LANES - 1, left[c + 1], left[c])
+                    sh[p, below, cs] = mid
+                    out[p, r, cs] = mid + AZIMUTH_COEF * (nxt + prev - 2.0 * mid)
+
+            numbers = [tile * SUB + s for s in range(SUB)]
+            shift_rows(numbers, row_offsets(numbers), source_ref, slot, write)
+
+        def pair(k, carry):
+            one(2 * k, 0)
+            one(2 * k + 1, 1)
+            return carry
+
+        lax.fori_loop(0, tiles // 2, pair, 0)
+
+    def send_edges(f):
+        ps = pl.ds(polar * f, polar)
+        got = []
+        for side in range(2):
+            c = remote(eo.at[side, ps], ei.at[1 - side, ps], rad_at(-1 if side == 0 else 1))
+            goes, comes = (inner, outer) if side == 0 else (outer, inner)
+            pl.when(goes)(c.start)
+            chained.append((goes, c))
+            got.append((comes, c))
+        return got
+
+    def take_edges(f, got):
+        for comes, c in got:
+            pl.when(comes)(c.wait_recv)
+        for h in range(polar):
+            p = polar * f + h
+            sh[p, SUB - 1:SUB, :] = jnp.where(rad > 0, ei[0, p], 0.0)
+            sh[p, SUB + rows:SUB + rows + 1, :] = jnp.where(rad < n_rad - 1, ei[1, p], 0.0)
+
+    def smooth(f, h):
+        p = polar * f + h
+        for tile in range(tiles):
+            top = SUB + tile * SUB
+            r = pl.ds(tile * SUB, SUB)
+            mid = sh[p, top:top + SUB, :]
+            up = sh[p, top - 1:top + SUB - 1, :]
+            down = sh[p, top + 1:top + SUB + 1, :]
+            new = out[p, r, :] + visc[h, r, :] * (down + up - 2.0 * mid)
+            if f == energy:
+                new = new + heat[h, r, :]
+            out[p, r, :] = new
+
+    def forward(f):
+        i = order.index(f)
+        onward = []
+        for c, lo, hi in zip(crossing[f], cuts[f], cuts[f][1:]):
+            c.wait_recv()
+            at = pl.ds(half + lo, hi - lo)
+            c = remote(pool_mine[f].at[at], pool_other[f].at[at], sibling)
+            c.start()
+            sent.append(c)
+            onward.append(c)
+        own_mine[i].wait()
+        to_mine[i].wait_recv()
+        return onward
+
+    def other_ready(f, onward):
+        i = order.index(f)
+        own_other[i].wait()
+        to_other[i].wait_recv()
+        for c in onward:
+            c.wait_recv()
+
+    def work(f):
+        onward = forward(f)
+        shift_plane(f, pool_mine[f], polar * f + core)
+        other_ready(f, onward)
+        shift_plane(f, pool_other[f], polar * f + 1 - core)
+        for h in range(polar):
+            p = polar * f + h
+            eo[0, p] = sh[p, SUB:SUB + 1, :]
+            eo[1, p] = sh[p, SUB + rows - 1:SUB + rows, :]
+        return send_edges(f)
+
+    def finish(f, got):
+        take_edges(f, got)
+        for h in range(polar):
+            smooth(f, h)
+
+    early_at = pl.ds(half, n_early)
+
+    def early_edges():
+        crossing_early.wait_recv()
+        onward = remote(early_mine.at[early_at], early_other.at[early_at], sibling)
+        onward.start()
+        sent.append(onward)
+        numbers = [0, rows - 1]
+        for c in own_early:
+            c.wait()
+        for c in to_early:
+            c.wait_recv()
+        copies = [local(early_mine.at[early_at], pool_mine[last].at[early_at])]
+        for ref, hh in ((early_mine, core), (early_other, 1 - core)):
+            p = polar * last + hh
+            if ref is early_other:
+                onward.wait_recv()
+                copies.append(local(early_other.at[early_at], pool_other[last].at[early_at]))
+
+            def write(x):
+                for c in range(cols):
+                    cs = pl.ds(c * LANES, LANES)
+                    eo[0, p, :, cs] = x[c + 1][:1]
+                    eo[1, p, :, cs] = x[c + 1][1:2]
+
+            shift_rows(numbers, row_offsets(numbers), ref, 0, write)
+        got = send_edges(last)
+        for c in copies:
+            c.wait()
+        return got
+
+    take_copy.wait()
+    pack_ready(dust)
+    pack_send(dust)
+    for c in to_pack[2:]:
+        c.start()
+    look_copy.wait()
+    pack_ready(energy)
+    pack_send(energy)
+    for i in range(2):
+        to_mine[i].start()
+        to_other[i].start()
+    for f in order[2:-1]:
+        pack_ready(f)
+        pack_send(f)
+    pack_ready(last)
+    pack([last], 0, n_early)
+    crossing_early = remote(packed[last].at[pl.ds(0, n_early)], early_mine.at[early_at], across)
+    crossing_early.start()
+    sent.append(crossing_early)
+    for c in to_early:
+        c.start()
+    for i in range(2, fields):
+        to_mine[i].start()
+        to_other[i].start()
+    pack_send(last)
+    for c in params:
+        c.wait()
+
+    finish(dust, work(dust))
+
+    row = lax.broadcasted_iota(jnp.int32, (SUB, width), 0)
+    for h in range(polar):
+        run_last = jnp.zeros((1, width), jnp.float32)
+        for t in range(tiles):
+            r = pl.ds(t * SUB, SUB)
+            step = 2.0 * absorb[h, r, :] * out[polar * dust + h, r, :] / total_rows
+            run = step
+            for k in (1, 2, 4):
+                run = run + jnp.where(row >= k, pltpu.roll(run, k, 0), 0.0)
+            run = run + run_last
+            depth[h, r, :] = run - 0.5 * step
+            run_last = run[SUB - 1:]
+        tot_out[0, h] = run_last
+    over = (used > cap).astype(jnp.float32)[:1]
+    for c in range(cols):
+        tot_out[0, polar, :, pl.ds(c * LANES, LANES)] = over
+
+    hops = []
+
+    def scan_send():
+        i = len(hops)
+        peer, upper = rad_pair(i)
+        c = remote(tot_out.at[i], tot_in.at[i], peer)
+        c.start()
+        sent.append(c)
+        hops.append((c, upper))
+
+    def scan_take():
+        i = len(hops) - 1
+        hops[i][0].wait_recv()
+        tot_out[i + 1] = tot_out[i] + tot_in[i]
+
+    scan_send()
+    pending = (energy, work(energy))
+    scan_take()
+    while len(hops) < n_scan:
+        scan_send()
+        scan_take()
+    for h in range(polar):
+        carried = jnp.where(hops[0][1] == 1, tot_in[0, h], 0.0)
+        for i in range(1, n_scan):
+            carried = carried + jnp.where(hops[i][1] == 1, tot_in[i, h], 0.0)
+        for t in range(tiles):
+            r = pl.ds(t * SUB, SUB)
+            radius = (rad * rows + t * SUB + row).astype(jnp.float32) + 0.5
+            flux = 1.0 / (1.0 + radius / total_rows)
+            depth[h, r, :] = depth[h, r, :] + carried
+            heat[h, r, :] = flux * jnp.exp(-depth[h, r, :])
+    flag[0] = jnp.max(tot_out[n_scan, polar])
+    for f in order[2:-1]:
+        following = (f, work(f))
+        finish(*pending)
+        pending = following
+    last_edges = early_edges()
+    finish(*pending)
+    take_edges(last, last_edges)
+    onward = forward(last)
+    shift_plane(last, pool_mine[last], polar * last + core)
+    smooth(last, core)
+    other_ready(last, onward)
+    shift_plane(last, pool_other[last], polar * last + 1 - core)
+    smooth(last, 1 - core)
+    for goes, c in chained:
+        pl.when(goes)(c.wait_send)
+    for c in sent:
+        c.wait_send()
+
+
+def fast(n_rad, n_az, state, offsets, viscosity, absorb):
+    fields, polar, rows, width = state.shape
+    planes = fields * polar
+    cols = width // LANES
+    units = rows * cols
+    cap = units * 2 * 23 // 32 // 16 * 16
+    n_early = 4 * cols
+    n_scan = (n_rad - 1).bit_length()
+    n_sems = 9 * fields + 4 + n_scan
+    f32, i32 = jnp.float32, jnp.int32
+    vm = pl.BlockSpec(memory_space=pltpu.VMEM)
+    sm = pl.BlockSpec(memory_space=pltpu.SMEM)
+    hbm = pl.BlockSpec(memory_space=pl.ANY)
+    source = state.reshape(planes, rows // SUB, SUB, cols, LANES).transpose(0, 1, 3, 2, 4).reshape(planes, units, LANES)
+    moved, local, flag = pl.pallas_call(
+        functools.partial(fast_kernel, n_rad, n_az, cap),
+        out_shape=(
+            pltpu.VMEM((planes, rows, width), f32),
+            pltpu.VMEM((polar, rows, width), f32),
+            jax.ShapeDtypeStruct((1,), f32),
+        ),
+        in_specs=[hbm, sm, hbm, hbm],
+        out_specs=(vm, vm, sm),
+        scratch_shapes=[
+            pltpu.VMEM((polar, rows, width), f32),
+            pltpu.VMEM((polar, rows, width), f32),
+            pltpu.VMEM((polar, rows, width), f32),
+            [pltpu.VMEM((2 * units, LANES), f32)] * fields,
+            [pltpu.VMEM((cap, LANES), f32)] * fields,
+            [pltpu.VMEM((2 * units + cap, LANES), f32)] * fields,
+            [pltpu.VMEM((2 * units + cap, LANES), f32)] * fields,
+            pltpu.VMEM((2 * units + n_early, LANES), f32),
+            pltpu.VMEM((2 * units + n_early, LANES), f32),
+            pltpu.VMEM((2, cols + 2, SUB, LANES), f32),
+            pltpu.VMEM((planes, rows + 2 * SUB, width), f32),
+            pltpu.VMEM((2, planes, 1, width), f32),
+            pltpu.VMEM((2, planes, 1, width), f32),
+            pltpu.VMEM((n_scan + 1, polar + 1, 1, width), f32),
+            pltpu.VMEM((n_scan, polar + 1, 1, width), f32),
+            pltpu.VMEM((SUB, LANES), i32),
+            pltpu.VMEM((rows, LANES), i32),
+            pltpu.SMEM((SUB, LANES), i32),
+            pltpu.SMEM((rows, LANES), i32),
+            pltpu.SemaphoreType.DMA((n_sems,)),
+            pltpu.SemaphoreType.DMA((n_sems,)),
+            pltpu.SemaphoreType.DMA((3 * fields + 8,)),
+        ],
+        compiler_params=pltpu.CompilerParams(
+            collective_id=1, has_side_effects=True, vmem_limit_bytes=40 * 2**20
+        ),
+    )(source, offsets, viscosity, absorb)
+    return moved, local, flag[0]
+
+
+def body(n_rad, n_az, state, offsets, viscosity, absorb):
+    args = (state, offsets, viscosity, absorb)
+    if n_az != 4 or state.shape[1] != 2 or n_rad < 2 or n_rad & (n_rad - 1):
+        moved, local = full(n_rad, n_az, *args)
+    else:
+        moved, local, flag = fast(n_rad, n_az, *args)
+        moved, local = lax.cond(
+            flag > 0, lambda m, d: tuple(full(n_rad, n_az, *args)), lambda m, d: (m, d), moved, local
+        )
+    return moved.reshape(state.shape), local
 
 
 def solution(mesh):

time: 46.1 us -> 44.9 us (0.974)
  Pallas kernels: 43.5 us -> 41.4 us
  between operations: 0.64 us -> 1.39 us
    pallas_call x1, Pallas kernels: 43.5 us -> 41.4 us  [fast(): pl.pallas_call(functools.partial(fast_kernel, n_rad, n_az, cap), out_shap...]
    unnamed x2 -> x10, local copies, waits for them, and re-layouts: 1.85 us -> 1.86 us
where the time goes in v2:
time: 44.9 us; the launch traced here: 44.7 us
  Pallas kernels  41.4 us (92%)
  local copies, waits for them, and re-layouts  1.86 us (4%)
  between operations  1.39 us (3%)
    pallas_call x1, Pallas kernels, fast(): pl.pallas_call(functools.partial(fast_kernel, n_rad, n_az, cap), out_shap...  41.4 us
    unnamed x10, local copies, waits for them, and re-layouts  1.86 us

profile of v2, /device:TPU:0, one launch (start us, length us, event | category | flops | bytes accessed | tf_op | source)
XLA Modules:
  0.0 44.7 jit_solution(13228184658158348059)
XLA Ops:
  0.6 0.0 copy-start.2
  0.6 0.0 copy-start.1
  0.7 0.0 copy-start.3
  0.7 0.0 copy-start
  0.7 41.4 %shard_map.59 = (f32[12,32,1024]{2,1,0:T(8,128)S(1)}, f32[2,32,1024]{2,1,0:T(8,128)S(1)}, f32[1]{0:T(128)}) custom-call(f32[12,256,128]{2,1,0:T(8,128)} %bitcast.9, s32[32]{0:T(128)} %offs.1, f32[2,32,1024]{2,1,0:T(8,128)} %visc_in.1, f32[2,32,1024]{2,1,0:T(8,128)} %absorb_in.1), custom_call_target="tpu_custom_call" | custom-call | tf_op jit(solution)/shard_map/pallas_call | solution.py:763
  42.8 0.0 copy-done.2
  42.8 0.0 copy-done.1
  42.8 0.0 copy-done.3
  42.8 0.0 copy-done
  42.9 1.1 %copy.12 = f32[6,2,32,1024]{3,2,1,0:T(8,128)} copy(f32[6,2,32,1024]{3,2,1,0:T(8,128)S(1)} %bitcast.8) | data formatting | bytes 3145728
  44.0 0.7 %copy.13 = f32[2,32,1024]{2,1,0:T(8,128)} copy(f32[2,32,1024]{2,1,0:T(8,128)S(1)} %get-tuple-element.47) | data formatting | bytes 524288
  (1 shorter events, 0.0 us)
Async XLA Ops:
  0.6 42.2 %copy-start.2 = (f32[2,32,1024]{2,1,0:T(8,128)S(1)}, f32[2,32,1024]{2,1,0:T(8,128)}, u32[]{:S(2)}) copy-start(f32[2,32,1024]{2,1,0:T(8,128)} %absorb_in.1) | copy-start | bytes 786436
  0.6 42.2 %copy-start.1 = (f32[2,32,1024]{2,1,0:T(8,128)S(1)}, f32[2,32,1024]{2,1,0:T(8,128)}, u32[]{:S(2)}) copy-start(f32[2,32,1024]{2,1,0:T(8,128)} %visc_in.1) | copy-start | bytes 786436
  0.7 42.2 %copy-start.3 = (s32[32]{0:T(128)S(1)}, s32[32]{0:T(128)}, u32[]{:S(2)}) copy-start(s32[32]{0:T(128)} %offs.1) | copy-start | bytes 388
  0.7 42.2 %copy-start = (f32[6,2,32,1024]{3,2,1,0:T(8,128)S(1)}, f32[6,2,32,1024]{3,2,1,0:T(8,128)}, u32[]{:S(2)}) copy-start(f32[6,2,32,1024]{3,2,1,0:T(8,128)} %param.6) | copy-start | bytes 4718596

commit v3 on v2

--- a/solution.py
+++ b/solution.py
@@ -417,15 +417,6 @@
     sent += to_pack + to_mine + to_other + to_early
     for c in to_pack[:2]:
         c.start()
-    own_pack = first_pack + [local(source.at[polar * f + core], gathered[f].at[mine]) for f in order[2:]]
-    own_mine = [local(source.at[polar * f + core], pool_mine[f].at[mine]) for f in order]
-    own_other = [local(source.at[polar * f + 1 - core], pool_other[f].at[mine]) for f in order]
-    own_early = [
-        local(source.at[polar * last + core], early_mine.at[mine]),
-        local(source.at[polar * last + 1 - core], early_other.at[mine]),
-    ]
-    params = [local(visc_in, visc), local(absorb_in, absorb)]
-
     lane = lax.broadcasted_iota(jnp.int32, (SUB, LANES), 1)
     sub = lax.broadcasted_iota(jnp.int32, (SUB, LANES), 0)
 
@@ -617,6 +608,15 @@
         for h in range(polar):
             smooth(f, h)
 
+    def flush(but=()):
+        for goes, c in chained:
+            pl.when(goes)(c.wait_send)
+        for c in sent:
+            if not any(c is b for b in but):
+                c.wait_send()
+        sent[:] = but
+        chained.clear()
+
     early_at = pl.ds(half, n_early)
 
     def early_edges():
@@ -648,31 +648,45 @@
             c.wait()
         return got
 
+    own_pack = first_pack
     take_copy.wait()
     pack_ready(dust)
     pack_send(dust)
+    own_pack = first_pack + [local(source.at[polar * f + core], gathered[f].at[mine]) for f in order[2:]]
     for c in to_pack[2:]:
         c.start()
     look_copy.wait()
     pack_ready(energy)
     pack_send(energy)
-    for i in range(2):
+    own_mine, own_other = [], []
+
+    def fill_pools(i):
+        f = order[i]
         to_mine[i].start()
         to_other[i].start()
-    for f in order[2:-1]:
-        pack_ready(f)
-        pack_send(f)
+        own_mine.append(local(source.at[polar * f + core], pool_mine[f].at[mine]))
+        own_other.append(local(source.at[polar * f + 1 - core], pool_other[f].at[mine]))
+
+    fill_pools(0)
+    params = [local(visc_in, visc), local(absorb_in, absorb)]
     pack_ready(last)
     pack([last], 0, n_early)
     crossing_early = remote(packed[last].at[pl.ds(0, n_early)], early_mine.at[early_at], across)
     crossing_early.start()
     sent.append(crossing_early)
+    for i in range(2, fields - 1):
+        pack_ready(order[i])
+        pack_send(order[i])
+        fill_pools(i - 1)
+    own_early = [
+        local(source.at[polar * last + core], early_mine.at[mine]),
+        local(source.at[polar * last + 1 - core], early_other.at[mine]),
+    ]
     for c in to_early:
         c.start()
-    for i in range(2, fields):
-        to_mine[i].start()
-        to_other[i].start()
     pack_send(last)
+    for i in range(fields - 2, fields):
+        fill_pools(i)
     for c in params:
         c.wait()
 
@@ -710,40 +724,48 @@
         hops[i][0].wait_recv()
         tot_out[i + 1] = tot_out[i] + tot_in[i]
 
+    def irradiate():
+        for h in range(polar):
+            carried = jnp.where(hops[0][1] == 1, tot_in[0, h], 0.0)
+            for i in range(1, n_scan):
+                carried = carried + jnp.where(hops[i][1] == 1, tot_in[i, h], 0.0)
+            for t in range(tiles):
+                r = pl.ds(t * SUB, SUB)
+                radius = (rad * rows + t * SUB + row).astype(jnp.float32) + 0.5
+                flux = 1.0 / (1.0 + radius / total_rows)
+                depth[h, r, :] = depth[h, r, :] + carried
+                heat[h, r, :] = flux * jnp.exp(-depth[h, r, :])
+        flag[0] = jnp.max(tot_out[n_scan, polar])
+
     scan_send()
-    pending = (energy, work(energy))
-    scan_take()
-    while len(hops) < n_scan:
-        scan_send()
-        scan_take()
-    for h in range(polar):
-        carried = jnp.where(hops[0][1] == 1, tot_in[0, h], 0.0)
-        for i in range(1, n_scan):
-            carried = carried + jnp.where(hops[i][1] == 1, tot_in[i, h], 0.0)
-        for t in range(tiles):
-            r = pl.ds(t * SUB, SUB)
-            radius = (rad * rows + t * SUB + row).astype(jnp.float32) + 0.5
-            flux = 1.0 / (1.0 + radius / total_rows)
-            depth[h, r, :] = depth[h, r, :] + carried
-            heat[h, r, :] = flux * jnp.exp(-depth[h, r, :])
-    flag[0] = jnp.max(tot_out[n_scan, polar])
-    for f in order[2:-1]:
-        following = (f, work(f))
-        finish(*pending)
-        pending = following
-    last_edges = early_edges()
-    finish(*pending)
+    pending = []
+    for f in order[1:-1]:
+        if f == order[2]:
+            last_edges = early_edges()
+        pending.append((f, work(f)))
+        if len(hops) < n_scan:
+            scan_take()
+            scan_send()
+            ready = [w for w in pending[:-1] if w[0] != energy]
+        else:
+            if energy in [w[0] for w in pending]:
+                scan_take()
+                irradiate()
+            ready = pending[:-1]
+        for w in ready:
+            finish(*w)
+            pending.remove(w)
     take_edges(last, last_edges)
+    flush(crossing[last])
     onward = forward(last)
+    for w in pending:
+        finish(*w)
     shift_plane(last, pool_mine[last], polar * last + core)
     smooth(last, core)
     other_ready(last, onward)
     shift_plane(last, pool_other[last], polar * last + 1 - core)
     smooth(last, 1 - core)
-    for goes, c in chained:
-        pl.when(goes)(c.wait_send)
-    for c in sent:
-        c.wait_send()
+    flush()
 
 
 def fast(n_rad, n_az, state, offsets, viscosity, absorb):
@@ -751,7 +773,7 @@
     planes = fields * polar
     cols = width // LANES
     units = rows * cols
-    cap = units * 2 * 23 // 32 // 16 * 16
+    cap = units * 2 * 11 // 16 // 16 * 16
     n_early = 4 * cols
     n_scan = (n_rad - 1).bit_length()
     n_sems = 9 * fields + 4 + n_scan
@@ -802,7 +824,7 @@
 
 def body(n_rad, n_az, state, offsets, viscosity, absorb):
     args = (state, offsets, viscosity, absorb)
-    if n_az != 4 or state.shape[1] != 2 or n_rad < 2 or n_rad & (n_rad - 1):
+    if n_az != 4 or state.shape[1] != 2 or n_rad not in (2, 4, 8, 16):
         moved, local = full(n_rad, n_az, *args)
     else:
         moved, local, flag = fast(n_rad, n_az, *args)

time: 44.9 us -> 40.4 us (0.90)
  Pallas kernels: 41.4 us -> 37 us
    pallas_call x1, Pallas kernels: 41.4 us -> 37 us  [fast(): pl.pallas_call(functools.partial(fast_kernel, n_rad, n_az, cap), out_shap...]
where the time goes in v3:
time: 40.4 us; the launch traced here: 40.2 us
  Pallas kernels  37 us (92%)
  local copies, waits for them, and re-layouts  1.86 us (5%)
  between operations  1.39 us (3%)
    pallas_call x1, Pallas kernels, fast(): pl.pallas_call(functools.partial(fast_kernel, n_rad, n_az, cap), out_shap...  37 us
    unnamed x10, local copies, waits for them, and re-layouts  1.86 us

profile of v3, /device:TPU:0, one launch (start us, length us, event | category | flops | bytes accessed | tf_op | source)
XLA Modules:
  0.0 40.2 jit_solution(14854835888615149285)
XLA Ops:
  0.6 0.0 copy-start.2
  0.6 0.0 copy-start.1
  0.7 0.0 copy-start.3
  0.7 0.0 copy-start
  0.7 37.0 %shard_map.59 = (f32[12,32,1024]{2,1,0:T(8,128)S(1)}, f32[2,32,1024]{2,1,0:T(8,128)S(1)}, f32[1]{0:T(128)}) custom-call(f32[12,256,128]{2,1,0:T(8,128)} %bitcast.9, s32[32]{0:T(128)} %offs.1, f32[2,32,1024]{2,1,0:T(8,128)} %visc_in.1, f32[2,32,1024]{2,1,0:T(8,128)} %absorb_in.1), custom_call_target="tpu_custom_call" | custom-call | tf_op jit(solution)/shard_map/pallas_call | solution.py:785
  38.3 0.0 copy-done.2
  38.3 0.0 copy-done.1
  38.3 0.0 copy-done.3
  38.3 0.0 copy-done
  38.4 1.1 %copy.12 = f32[6,2,32,1024]{3,2,1,0:T(8,128)} copy(f32[6,2,32,1024]{3,2,1,0:T(8,128)S(1)} %bitcast.8) | data formatting | bytes 3145728
  39.5 0.7 %copy.13 = f32[2,32,1024]{2,1,0:T(8,128)} copy(f32[2,32,1024]{2,1,0:T(8,128)S(1)} %get-tuple-element.47) | data formatting | bytes 524288
  (1 shorter events, 0.0 us)
Async XLA Ops:
  0.6 37.7 %copy-start.2 = (f32[2,32,1024]{2,1,0:T(8,128)S(1)}, f32[2,32,1024]{2,1,0:T(8,128)}, u32[]{:S(2)}) copy-start(f32[2,32,1024]{2,1,0:T(8,128)} %absorb_in.1) | copy-start | bytes 786436
  0.6 37.7 %copy-start.1 = (f32[2,32,1024]{2,1,0:T(8,128)S(1)}, f32[2,32,1024]{2,1,0:T(8,128)}, u32[]{:S(2)}) copy-start(f32[2,32,1024]{2,1,0:T(8,128)} %visc_in.1) | copy-start | bytes 786436
  0.7 37.7 %copy-start.3 = (s32[32]{0:T(128)S(1)}, s32[32]{0:T(128)}, u32[]{:S(2)}) copy-start(s32[32]{0:T(128)} %offs.1) | copy-start | bytes 388
  0.7 37.7 %copy-start = (f32[6,2,32,1024]{3,2,1,0:T(8,128)S(1)}, f32[6,2,32,1024]{3,2,1,0:T(8,128)}, u32[]{:S(2)}) copy-start(f32[6,2,32,1024]{3,2,1,0:T(8,128)} %param.6) | copy-start | bytes 4718596

commit v4 on v3

--- a/solution.py
+++ b/solution.py
@@ -340,9 +340,9 @@
     return moved, local
 
 
-def fast_kernel(n_rad, n_az, cap, source, offs, visc_in, absorb_in, out, depth, flag,
+def fast_kernel(n_rad, n_az, cap, source, offs_in, visc_in, absorb_in, out, depth, flag,
                 visc, absorb, heat, gathered, packed, pool_mine, pool_other, early_mine, early_other,
-                stage, sh, eo, ei, tot_out, tot_in, take_v, look_v, take, look, ss, rs, ls):
+                stage, sh, eo, ei, tot_out, tot_in, take_v, look_v, take, look, offs, ss, rs, ls):
     rad = lax.axis_index("rad")
     az = lax.axis_index("az")
     core = lax.rem(az, 2)
@@ -391,6 +391,7 @@
         c.start()
         return c
 
+    offs_copy = local(offs_in, offs)
     inner, outer = rad > 0, rad < n_rad - 1
     ei[...] = jnp.zeros_like(ei)
     barrier = pltpu.get_barrier_semaphore()
@@ -429,6 +430,7 @@
     def block_unit(b):
         return (b >> col_bits) * units + (b & (cols - 1)) * SUB
 
+    offs_copy.wait()
     shifts = [row_offsets([t * SUB + k for k in range(SUB)]) for t in range(tiles)]
     leads, manys, befores = [], [], []
     used = jnp.zeros((SUB, LANES), jnp.int32)
@@ -779,7 +781,6 @@
     n_sems = 9 * fields + 4 + n_scan
     f32, i32 = jnp.float32, jnp.int32
     vm = pl.BlockSpec(memory_space=pltpu.VMEM)
-    sm = pl.BlockSpec(memory_space=pltpu.SMEM)
     hbm = pl.BlockSpec(memory_space=pl.ANY)
     source = state.reshape(planes, rows // SUB, SUB, cols, LANES).transpose(0, 1, 3, 2, 4).reshape(planes, units, LANES)
     moved, local, flag = pl.pallas_call(
@@ -787,10 +788,10 @@
         out_shape=(
             pltpu.VMEM((planes, rows, width), f32),
             pltpu.VMEM((polar, rows, width), f32),
-            jax.ShapeDtypeStruct((1,), f32),
+            pltpu.SMEM((1,), f32),
         ),
-        in_specs=[hbm, sm, hbm, hbm],
-        out_specs=(vm, vm, sm),
+        in_specs=[hbm, hbm, hbm, hbm],
+        out_specs=(vm, vm, pl.BlockSpec(memory_space=pltpu.SMEM)),
         scratch_shapes=[
             pltpu.VMEM((polar, rows, width), f32),
             pltpu.VMEM((polar, rows, width), f32),
@@ -811,15 +812,35 @@
             pltpu.VMEM((rows, LANES), i32),
             pltpu.SMEM((SUB, LANES), i32),
             pltpu.SMEM((rows, LANES), i32),
+            pltpu.SMEM((rows,), i32),
             pltpu.SemaphoreType.DMA((n_sems,)),
             pltpu.SemaphoreType.DMA((n_sems,)),
-            pltpu.SemaphoreType.DMA((3 * fields + 8,)),
+            pltpu.SemaphoreType.DMA((3 * fields + 10,)),
         ],
         compiler_params=pltpu.CompilerParams(
-            collective_id=1, has_side_effects=True, vmem_limit_bytes=40 * 2**20
+            collective_id=1, has_side_effects=True, vmem_limit_bytes=61 * 2**20
         ),
     )(source, offsets, viscosity, absorb)
     return moved, local, flag[0]
+
+
+def hand_out(moved, local):
+    def store(a, b, x, y, sems):
+        copies = [pltpu.make_async_copy(a, x, sems.at[0]), pltpu.make_async_copy(b, y, sems.at[1])]
+        for c in copies:
+            c.start()
+        for c in copies:
+            c.wait()
+
+    hbm = pl.BlockSpec(memory_space=pl.ANY)
+    vm = pl.BlockSpec(memory_space=pltpu.VMEM)
+    return pl.pallas_call(
+        store,
+        out_shape=(pltpu.HBM(moved.shape, moved.dtype), pltpu.HBM(local.shape, local.dtype)),
+        in_specs=[vm, vm],
+        out_specs=(hbm, hbm),
+        scratch_shapes=[pltpu.SemaphoreType.DMA((2,))],
+    )(moved, local)
 
 
 def body(n_rad, n_az, state, offsets, viscosity, absorb):
@@ -831,6 +852,7 @@
         moved, local = lax.cond(
             flag > 0, lambda m, d: tuple(full(n_rad, n_az, *args)), lambda m, d: (m, d), moved, local
         )
+    moved, local = hand_out(moved, local)
     return moved.reshape(state.shape), local
 
 

time: 40.4 us -> 37.8 us (0.936)
  local copies, waits for them, and re-layouts: 1.86 us -> 0.01 us
  between operations: 1.39 us -> 0.7 us
    unnamed x10 -> x6, local copies, waits for them, and re-layouts: 1.86 us -> 0.01 us
    pallas_call x1, Pallas kernels: 37 us -> 35.7 us  [fast(): pl.pallas_call(functools.partial(fast_kernel, n_rad, n_az, cap), out_shap...]
    pallas_call x0 -> x1, Pallas kernels: none -> 1.24 us  [hand_out(): pl.pallas_call(store, out_shape=(pltpu.HBM(moved.shape, moved.dtype), plt...]
where the time goes in v4:
time: 37.8 us; the launch traced here: 37.6 us
  Pallas kernels  36.9 us (98%)
  between operations  0.7 us (2%)
    pallas_call x1, Pallas kernels, fast(): pl.pallas_call(functools.partial(fast_kernel, n_rad, n_az, cap), out_shap...  35.7 us
    pallas_call x1, Pallas kernels, hand_out(): pl.pallas_call(store, out_shape=(pltpu.HBM(moved.shape, moved.dtype), plt...  1.24 us

profile of v4, /device:TPU:0, one launch (start us, length us, event | category | flops | bytes accessed | tf_op | source)
XLA Modules:
  0.0 37.6 jit_solution(13990440126612989851)
XLA Ops:
  0.6 0.0 copy-start.1
  0.6 0.0 copy-start
  0.7 0.0 copy-start.2
  0.7 35.7 %shard_map.59 = (f32[12,32,1024]{2,1,0:T(8,128)S(1)}, f32[2,32,1024]{2,1,0:T(8,128)S(1)}, f32[1]{0:T(128)S(4)}) custom-call(f32[12,256,128]{2,1,0:T(8,128)} %bitcast.8, s32[32]{0:T(128)} %offs_in.1, f32[2,32,1024]{2,1,0:T(8,128)} %visc_in.1, f32[2,32,1024]{2,1,0:T(8,128)} %absorb_in.1), custom_call_target="tpu_custom_call" | custom-call | tf_op jit(solution)/shard_map/pallas_call | solution.py:786
  36.3 0.0 copy-done.1
  36.3 0.0 copy-done
  36.4 0.0 copy-done.2
  36.4 1.2 %shard_map.60 = (f32[12,32,1024]{2,1,0:T(8,128)}, f32[2,32,1024]{2,1,0:T(8,128)}) custom-call(f32[12,32,1024]{2,1,0:T(8,128)S(1)} %get-tuple-element.28.a, f32[2,32,1024]{2,1,0:T(8,128)S(1)} %get-tuple-element.29.b), custom_call_target="tpu_custom_call" | custom-call | tf_op jit(solution)/shard_map/pallas_call | solution.py:837
  (1 shorter events, 0.0 us)
Async XLA Ops:
  0.6 35.7 %copy-start.1 = (f32[2,32,1024]{2,1,0:T(8,128)S(1)}, f32[2,32,1024]{2,1,0:T(8,128)}, u32[]{:S(2)}) copy-start(f32[2,32,1024]{2,1,0:T(8,128)} %absorb_in.1) | copy-start | bytes 786436
  0.6 35.7 %copy-start = (f32[2,32,1024]{2,1,0:T(8,128)S(1)}, f32[2,32,1024]{2,1,0:T(8,128)}, u32[]{:S(2)}) copy-start(f32[2,32,1024]{2,1,0:T(8,128)} %visc_in.1) | copy-start | bytes 786436
  0.7 35.7 %copy-start.2 = (s32[32]{0:T(128)S(1)}, s32[32]{0:T(128)}, u32[]{:S(2)}) copy-start(s32[32]{0:T(128)} %offs_in.1) | copy-start | bytes 388

commit v5 on v4

--- a/solution.py
+++ b/solution.py
@@ -340,7 +340,7 @@
     return moved, local
 
 
-def fast_kernel(n_rad, n_az, cap, source, offs_in, visc_in, absorb_in, out, depth, flag,
+def fast_kernel(n_rad, n_az, cap, dust_cap, source, offs_in, visc_in, absorb_in, out, depth, flag,
                 visc, absorb, heat, gathered, packed, pool_mine, pool_other, early_mine, early_other,
                 stage, sh, eo, ei, tot_out, tot_in, take_v, look_v, take, look, offs, ss, rs, ls):
     rad = lax.axis_index("rad")
@@ -365,6 +365,9 @@
     last = order[-1]
     n_scan = (n_rad - 1).bit_length()
     n_early = 2 * ring
+    n_raw = SUB * cols
+    raw_at = half + cap
+    take_rows = -(-cap // LANES)
 
     def rad_at(k):
         return {"rad": lax.rem(rad + k + n_rad, n_rad)}
@@ -403,7 +406,7 @@
             pl.semaphore_signal(barrier, inc=1, device_id=rad_at(k), device_id_type=pl.DeviceIdType.MESH)
 
     mine = pl.ds(core * units, units)
-    first_pack = [local(source.at[polar * f + core], gathered[f].at[mine]) for f in order[:2]]
+    first_pack = [local(source.at[polar * f + core], gathered[f].at[mine]) for f in order[:1]]
 
     pl.semaphore_wait(barrier, 2 + n_scan - 1 + inner.astype(jnp.int32) + outer.astype(jnp.int32))
 
@@ -416,8 +419,18 @@
         remote(source.at[polar * last + core], early_other.at[mine], sibling),
     ]
     sent += to_pack + to_mine + to_other + to_early
-    for c in to_pack[:2]:
+    to_pack[0].start()
+    raw_mine = remote(
+        source.at[polar * dust + core, pl.ds(0, n_raw)],
+        pool_mine[dust].at[pl.ds(raw_at + core * n_raw, n_raw)], across,
+    )
+    raw_other = remote(
+        source.at[polar * dust + 1 - core, pl.ds(0, n_raw)],
+        pool_other[dust].at[pl.ds(raw_at + core * n_raw, n_raw)], across,
+    )
+    for c in (raw_mine, raw_other):
         c.start()
+        sent.append(c)
     lane = lax.broadcasted_iota(jnp.int32, (SUB, LANES), 1)
     sub = lax.broadcasted_iota(jnp.int32, (SUB, LANES), 0)
 
@@ -455,34 +468,46 @@
         if t == tiles - 1:
             base = jnp.where(sub == SUB - 1, top_many, base)
         bases.append(base)
-    for q in range(-(-cap // LANES)):
-        j = q * LANES + lane
-        place = jnp.zeros((SUB, LANES), jnp.int32)
-        ahead = jnp.zeros((SUB, LANES), jnp.int32)
-        for t in range(tiles):
-            held = (j >= bases[t]) & (j < bases[t] + manys[t])
-            place = place + jnp.where(held, t * SUB * cols + sub, 0)
-            ahead = ahead + jnp.where(held, leads[t] - bases[t], 0)
-        for k in (4, 2, 1):
-            place = place + pltpu.roll(place, k, 0)
-            ahead = ahead + pltpu.roll(ahead, k, 0)
-        take_v[q:q + 1, :] = (block_unit((j + ahead) & (ring - 1)) + place)[:1]
+    top_used = befores[1]
+    top_used = jnp.broadcast_to(top_used[:1], (SUB, LANES))
+    dust_bases = [None] + [before - top_used for before in befores[1:]]
+    for size, heads, first, at in ((dust_cap, dust_bases, 1, take_rows), (cap, bases, 0, 0)):
+        for q in range(-(-size // LANES)):
+            j = q * LANES + lane
+            place = jnp.zeros((SUB, LANES), jnp.int32)
+            ahead = jnp.zeros((SUB, LANES), jnp.int32)
+            for t in range(first, tiles):
+                held = (j >= heads[t]) & (j < heads[t] + manys[t])
+                place = place + jnp.where(held, t * SUB * cols + sub, 0)
+                ahead = ahead + jnp.where(held, leads[t] - heads[t], 0)
+            for k in (4, 2, 1):
+                place = place + pltpu.roll(place, k, 0)
+                ahead = ahead + pltpu.roll(ahead, k, 0)
+            take_v[at + q:at + q + 1, :] = (block_unit((j + ahead) & (ring - 1)) + place)[:1]
     take_copy = local(take_v, take)
     for t in range(tiles):
         b = az * cols - (shifts[t] >> LANE_BITS) - 1 + lane + 2 * ring
         near = block_unit(b & (ring - 1)) + (t * SUB * cols + sub)
-        far = half + jnp.minimum(bases[t] + ((b - leads[t]) & (ring - 1)), cap - 1)
-        look_v[t * SUB:(t + 1) * SUB, :] = jnp.where(((b >> (col_bits + 1)) & 1) == chip, near, far)
+        here = ((b >> (col_bits + 1)) & 1) == chip
+        step = (b - leads[t]) & (ring - 1)
+        far = half + jnp.minimum(bases[t] + step, cap - 1)
+        look_v[t * SUB:(t + 1) * SUB, :] = jnp.where(here, near, far)
+        if t == 0:
+            far = raw_at + ((b & (ring - 1)) >> col_bits) * n_raw + (b & (cols - 1)) * SUB + sub
+        else:
+            far = half + jnp.minimum(dust_bases[t] + step, dust_cap - 1)
+        look_v[rows + t * SUB:rows + (t + 1) * SUB, :] = jnp.where(here, near, far)
     look_copy = local(look_v, look)
 
     crossing = {f: [] for f in order}
     cuts = {f: [0, cap // 2 // SUB * SUB, cap] for f in order}
+    cuts[dust] = [0, dust_cap // 4 // SUB * SUB, dust_cap * 5 // 8 // SUB * SUB, dust_cap]
     cuts[last] = [n_early, (n_early + cap) // 2 // SUB * SUB, cap]
 
     def pack(some, lo, hi):
         def eight(k, carry):
             for s in range(SUB):
-                u = take[k >> 4, (k & 15) * SUB + s]
+                u = take[(k >> 4) + (take_rows if some[0] == dust else 0), (k & 15) * SUB + s]
                 for f in some:
                     packed[f][pl.ds(k * SUB + s, 1), :] = gathered[f][pl.ds(u, 1), :]
             return carry
@@ -501,10 +526,10 @@
             sent.append(c)
             crossing[f].append(c)
 
-    def shift_rows(numbers, shift, source_ref, slot, write):
+    def shift_rows(f, numbers, shift, source_ref, slot, write):
         for s, r in enumerate(numbers):
             for i in range(span):
-                u = look[r, i]
+                u = look[r + (rows if f == dust else 0), i]
                 stage[slot, i, s:s + 1, :] = source_ref[pl.ds(u, 1), :]
         rem = shift & (LANES - 1)
         pick = (lane - rem) & (LANES - 1)
@@ -516,9 +541,9 @@
         write(x)
 
     def shift_plane(f, source_ref, p):
-        def one(tile, slot):
-            r = pl.ds(pl.multiple_of(tile * SUB, SUB), SUB)
-            below = pl.ds(pl.multiple_of(SUB + tile * SUB, SUB), SUB)
+        def one(tile):
+            r = pl.ds(tile * SUB, SUB)
+            below = pl.ds(SUB + tile * SUB, SUB)
 
             def write(x):
                 right = [pltpu.roll(v, 1, 1) for v in x[:-1]]
@@ -532,14 +557,10 @@
                     out[p, r, cs] = mid + AZIMUTH_COEF * (nxt + prev - 2.0 * mid)
 
             numbers = [tile * SUB + s for s in range(SUB)]
-            shift_rows(numbers, row_offsets(numbers), source_ref, slot, write)
-
-        def pair(k, carry):
-            one(2 * k, 0)
-            one(2 * k + 1, 1)
-            return carry
-
-        lax.fori_loop(0, tiles // 2, pair, 0)
+            shift_rows(f, numbers, row_offsets(numbers), source_ref, tile, write)
+
+        for t in range(tiles):
+            one(t)
 
     def send_edges(f):
         ps = pl.ds(polar * f, polar)
@@ -644,7 +665,7 @@
                     eo[0, p, :, cs] = x[c + 1][:1]
                     eo[1, p, :, cs] = x[c + 1][1:2]
 
-            shift_rows(numbers, row_offsets(numbers), ref, 0, write)
+            shift_rows(last, numbers, row_offsets(numbers), ref, 0, write)
         got = send_edges(last)
         for c in copies:
             c.wait()
@@ -652,14 +673,23 @@
 
     own_pack = first_pack
     take_copy.wait()
+    to_pack[1].start()
     pack_ready(dust)
     pack_send(dust)
-    own_pack = first_pack + [local(source.at[polar * f + core], gathered[f].at[mine]) for f in order[2:]]
+    own_pack = first_pack + [local(source.at[polar * f + core], gathered[f].at[mine]) for f in order[1:]]
     for c in to_pack[2:]:
         c.start()
     look_copy.wait()
     pack_ready(energy)
     pack_send(energy)
+    raw_here = pl.ds(raw_at + core * n_raw, n_raw)
+    raw_onward = []
+    for c, src, dst in ((raw_mine, pool_mine, pool_other), (raw_other, pool_other, pool_mine)):
+        c.wait_recv()
+        c = remote(src[dust].at[raw_here], dst[dust].at[raw_here], sibling)
+        c.start()
+        sent.append(c)
+        raw_onward.append(c)
     own_mine, own_other = [], []
 
     def fill_pools(i):
@@ -692,6 +722,8 @@
     for c in params:
         c.wait()
 
+    for c in raw_onward:
+        c.wait_recv()
     finish(dust, work(dust))
 
     row = lax.broadcasted_iota(jnp.int32, (SUB, width), 0)
@@ -707,7 +739,7 @@
             depth[h, r, :] = run - 0.5 * step
             run_last = run[SUB - 1:]
         tot_out[0, h] = run_last
-    over = (used > cap).astype(jnp.float32)[:1]
+    over = ((used > cap) | (used - top_used > dust_cap)).astype(jnp.float32)[:1]
     for c in range(cols):
         tot_out[0, polar, :, pl.ds(c * LANES, LANES)] = over
 
@@ -776,15 +808,18 @@
     cols = width // LANES
     units = rows * cols
     cap = units * 2 * 11 // 16 // 16 * 16
+    dust_cap = (units - SUB * cols) * 2 * 73 // 100 // SUB * SUB
     n_early = 4 * cols
+    n_take = -(-(-(-cap // LANES) - (-dust_cap // LANES)) // SUB) * SUB
     n_scan = (n_rad - 1).bit_length()
-    n_sems = 9 * fields + 4 + n_scan
+    n_sems = 9 * fields + 2 + 4 + 4 + n_scan
+    pools = [2 * units + cap] * (fields - 1) + [2 * units + cap + 2 * SUB * cols]
     f32, i32 = jnp.float32, jnp.int32
     vm = pl.BlockSpec(memory_space=pltpu.VMEM)
     hbm = pl.BlockSpec(memory_space=pl.ANY)
     source = state.reshape(planes, rows // SUB, SUB, cols, LANES).transpose(0, 1, 3, 2, 4).reshape(planes, units, LANES)
     moved, local, flag = pl.pallas_call(
-        functools.partial(fast_kernel, n_rad, n_az, cap),
+        functools.partial(fast_kernel, n_rad, n_az, cap, dust_cap),
         out_shape=(
             pltpu.VMEM((planes, rows, width), f32),
             pltpu.VMEM((polar, rows, width), f32),
@@ -798,20 +833,20 @@
             pltpu.VMEM((polar, rows, width), f32),
             [pltpu.VMEM((2 * units, LANES), f32)] * fields,
             [pltpu.VMEM((cap, LANES), f32)] * fields,
-            [pltpu.VMEM((2 * units + cap, LANES), f32)] * fields,
-            [pltpu.VMEM((2 * units + cap, LANES), f32)] * fields,
+            [pltpu.VMEM((n, LANES), f32) for n in pools],
+            [pltpu.VMEM((n, LANES), f32) for n in pools],
             pltpu.VMEM((2 * units + n_early, LANES), f32),
             pltpu.VMEM((2 * units + n_early, LANES), f32),
-            pltpu.VMEM((2, cols + 2, SUB, LANES), f32),
+            pltpu.VMEM((rows // SUB, cols + 2, SUB, LANES), f32),
             pltpu.VMEM((planes, rows + 2 * SUB, width), f32),
             pltpu.VMEM((2, planes, 1, width), f32),
             pltpu.VMEM((2, planes, 1, width), f32),
             pltpu.VMEM((n_scan + 1, polar + 1, 1, width), f32),
             pltpu.VMEM((n_scan, polar + 1, 1, width), f32),
-            pltpu.VMEM((SUB, LANES), i32),
-            pltpu.VMEM((rows, LANES), i32),
-            pltpu.SMEM((SUB, LANES), i32),
-            pltpu.SMEM((rows, LANES), i32),
+            pltpu.VMEM((n_take, LANES), i32),
+            pltpu.VMEM((2 * rows, LANES), i32),
+            pltpu.SMEM((n_take, LANES), i32),
+            pltpu.SMEM((2 * rows, LANES), i32),
             pltpu.SMEM((rows,), i32),
             pltpu.SemaphoreType.DMA((n_sems,)),
             pltpu.SemaphoreType.DMA((n_sems,)),

time: 37.8 us -> 36 us (0.952)
  Pallas kernels: 36.9 us -> 35.1 us
    pallas_call x1, Pallas kernels: 35.7 us -> 33.9 us  [fast(): pl.pallas_call(functools.partial(fast_kernel, n_rad, n_az, cap, dust_cap)...]
where the time goes in v5:
time: 36 us; the launch traced here: 35.8 us
  Pallas kernels  35.1 us (98%)
  between operations  0.7 us (2%)
    pallas_call x1, Pallas kernels, fast(): pl.pallas_call(functools.partial(fast_kernel, n_rad, n_az, cap, dust_cap)...  33.9 us
    pallas_call x1, Pallas kernels, hand_out(): pl.pallas_call(store, out_shape=(pltpu.HBM(moved.shape, moved.dtype), plt...  1.24 us

profile of v5, /device:TPU:0, one launch (start us, length us, event | category | flops | bytes accessed | tf_op | source)
XLA Modules:
  0.0 35.8 jit_solution(1041652390045779064)
XLA Ops:
  0.6 0.0 copy-start.1
  0.6 0.0 copy-start
  0.7 0.0 copy-start.2
  0.7 33.9 %shard_map.59 = (f32[12,32,1024]{2,1,0:T(8,128)S(1)}, f32[2,32,1024]{2,1,0:T(8,128)S(1)}, f32[1]{0:T(128)S(4)}) custom-call(f32[12,256,128]{2,1,0:T(8,128)} %bitcast.8, s32[32]{0:T(128)} %offs_in.1, f32[2,32,1024]{2,1,0:T(8,128)} %visc_in.1, f32[2,32,1024]{2,1,0:T(8,128)} %absorb_in.1), custom_call_target="tpu_custom_call" | custom-call | tf_op jit(solution)/shard_map/pallas_call | solution.py:821
  34.5 0.0 copy-done.1
  34.6 0.0 copy-done
  34.6 0.0 copy-done.2
  34.6 1.2 %shard_map.60 = (f32[12,32,1024]{2,1,0:T(8,128)}, f32[2,32,1024]{2,1,0:T(8,128)}) custom-call(f32[12,32,1024]{2,1,0:T(8,128)S(1)} %get-tuple-element.28.a, f32[2,32,1024]{2,1,0:T(8,128)S(1)} %get-tuple-element.29.b), custom_call_target="tpu_custom_call" | custom-call | tf_op jit(solution)/shard_map/pallas_call | solution.py:872
  (1 shorter events, 0.0 us)
Async XLA Ops:
  0.6 33.9 %copy-start.1 = (f32[2,32,1024]{2,1,0:T(8,128)S(1)}, f32[2,32,1024]{2,1,0:T(8,128)}, u32[]{:S(2)}) copy-start(f32[2,32,1024]{2,1,0:T(8,128)} %absorb_in.1) | copy-start | bytes 786436
  0.6 33.9 %copy-start = (f32[2,32,1024]{2,1,0:T(8,128)S(1)}, f32[2,32,1024]{2,1,0:T(8,128)}, u32[]{:S(2)}) copy-start(f32[2,32,1024]{2,1,0:T(8,128)} %visc_in.1) | copy-start | bytes 786436
  0.7 33.9 %copy-start.2 = (s32[32]{0:T(128)S(1)}, s32[32]{0:T(128)}, u32[]{:S(2)}) copy-start(s32[32]{0:T(128)} %offs_in.1) | copy-start | bytes 388

commit v6 on v5

--- a/solution.py
+++ b/solution.py
@@ -396,14 +396,19 @@
 
     offs_copy = local(offs_in, offs)
     inner, outer = rad > 0, rad < n_rad - 1
-    ei[...] = jnp.zeros_like(ei)
     barrier = pltpu.get_barrier_semaphore()
-    for peer in [sibling, across] + [rad_pair(i)[0] for i in range(1, n_scan)]:
+    for peer in [rad_pair(i)[0] for i in reversed(range(1, n_scan))]:
         pl.semaphore_signal(barrier, inc=1, device_id=peer, device_id_type=pl.DeviceIdType.MESH)
     for there, k in ((inner, -1), (outer, 1)):
         @pl.when(there)
         def _():
             pl.semaphore_signal(barrier, inc=1, device_id=rad_at(k), device_id_type=pl.DeviceIdType.MESH)
+    for peer in [sibling, across]:
+        pl.semaphore_signal(barrier, inc=1, device_id=peer, device_id_type=pl.DeviceIdType.MESH)
+    for edge, k in ((rad == 0, 0), (rad == n_rad - 1, 1)):
+        @pl.when(edge)
+        def _():
+            ei[k] = jnp.zeros(ei.shape[1:], jnp.float32)
 
     mine = pl.ds(core * units, units)
     first_pack = [local(source.at[polar * f + core], gathered[f].at[mine]) for f in order[:1]]
@@ -792,13 +797,13 @@
     take_edges(last, last_edges)
     flush(crossing[last])
     onward = forward(last)
-    for w in pending:
-        finish(*w)
     shift_plane(last, pool_mine[last], polar * last + core)
     smooth(last, core)
     other_ready(last, onward)
     shift_plane(last, pool_other[last], polar * last + 1 - core)
     smooth(last, 1 - core)
+    for w in pending:
+        finish(*w)
     flush()
 
 

time: 36 us -> 35.3 us (0.981)
  Pallas kernels: 35.1 us -> 34.5 us
    pallas_call x1, Pallas kernels: 33.9 us -> 33.2 us  [fast(): pl.pallas_call(functools.partial(fast_kernel, n_rad, n_az, cap, dust_cap)...]
where the time goes in v6:
time: 35.3 us; the launch traced here: 35.2 us
  Pallas kernels  34.5 us (98%)
  between operations  0.7 us (2%)
    pallas_call x1, Pallas kernels, fast(): pl.pallas_call(functools.partial(fast_kernel, n_rad, n_az, cap, dust_cap)...  33.2 us
    pallas_call x1, Pallas kernels, hand_out(): pl.pallas_call(store, out_shape=(pltpu.HBM(moved.shape, moved.dtype), plt...  1.24 us

profile of v6, /device:TPU:0, one launch (start us, length us, event | category | flops | bytes accessed | tf_op | source)
XLA Modules:
  0.0 35.2 jit_solution(7857130381957955111)
XLA Ops:
  0.6 0.0 copy-start.1
  0.6 0.0 copy-start
  0.7 0.0 copy-start.2
  0.7 33.2 %shard_map.59 = (f32[12,32,1024]{2,1,0:T(8,128)S(1)}, f32[2,32,1024]{2,1,0:T(8,128)S(1)}, f32[1]{0:T(128)S(4)}) custom-call(f32[12,256,128]{2,1,0:T(8,128)} %bitcast.8, s32[32]{0:T(128)} %offs_in.1, f32[2,32,1024]{2,1,0:T(8,128)} %visc_in.1, f32[2,32,1024]{2,1,0:T(8,128)} %absorb_in.1), custom_call_target="tpu_custom_call" | custom-call | tf_op jit(solution)/shard_map/pallas_call | solution.py:826
  33.9 0.0 copy-done.1
  33.9 0.0 copy-done
  33.9 0.0 copy-done.2
  34.0 1.2 %shard_map.60 = (f32[12,32,1024]{2,1,0:T(8,128)}, f32[2,32,1024]{2,1,0:T(8,128)}) custom-call(f32[12,32,1024]{2,1,0:T(8,128)S(1)} %get-tuple-element.28.a, f32[2,32,1024]{2,1,0:T(8,128)S(1)} %get-tuple-element.29.b), custom_call_target="tpu_custom_call" | custom-call | tf_op jit(solution)/shard_map/pallas_call | solution.py:877
  (1 shorter events, 0.0 us)
Async XLA Ops:
  0.6 33.3 %copy-start.1 = (f32[2,32,1024]{2,1,0:T(8,128)S(1)}, f32[2,32,1024]{2,1,0:T(8,128)}, u32[]{:S(2)}) copy-start(f32[2,32,1024]{2,1,0:T(8,128)} %absorb_in.1) | copy-start | bytes 786436
  0.6 33.3 %copy-start = (f32[2,32,1024]{2,1,0:T(8,128)S(1)}, f32[2,32,1024]{2,1,0:T(8,128)}, u32[]{:S(2)}) copy-start(f32[2,32,1024]{2,1,0:T(8,128)} %visc_in.1) | copy-start | bytes 786436
  0.7 33.3 %copy-start.2 = (s32[32]{0:T(128)S(1)}, s32[32]{0:T(128)}, u32[]{:S(2)}) copy-start(s32[32]{0:T(128)} %offs_in.1) | copy-start | bytes 388

commit v7 on v6

--- a/solution.py
+++ b/solution.py
@@ -532,15 +532,19 @@
             crossing[f].append(c)
 
     def shift_rows(f, numbers, shift, source_ref, slot, write):
-        for s, r in enumerate(numbers):
-            for i in range(span):
+        shown = []
+        for i in range(span):
+            value = None
+            for s, r in enumerate(numbers):
                 u = look[r + (rows if f == dust else 0), i]
-                stage[slot, i, s:s + 1, :] = source_ref[pl.ds(u, 1), :]
+                strip = jnp.broadcast_to(source_ref[pl.ds(u, 1), :], (SUB, LANES))
+                value = strip if s == 0 else jnp.where(sub == s, strip, value)
+            shown.append(value)
         rem = shift & (LANES - 1)
         pick = (lane - rem) & (LANES - 1)
         low = lane < rem
         turned = [
-            jnp.take_along_axis(stage[slot, i], pick, axis=1, mode="promise_in_bounds") for i in range(span)
+            jnp.take_along_axis(shown[i], pick, axis=1, mode="promise_in_bounds") for i in range(span)
         ]
         x = [turned[0]] + [jnp.where(low, turned[j - 1], turned[j]) for j in range(1, span)]
         write(x)

time: 35.3 us -> 35.3 us (level)
  no operation moved by 1% of the time
where the time goes in v7:
time: 35.3 us; the launch traced here: 35.1 us
  Pallas kernels  34.4 us (97%)
  between operations  0.7 us (2%)
    pallas_call x1, Pallas kernels, fast(): pl.pallas_call(functools.partial(fast_kernel, n_rad, n_az, cap, dust_cap)...  33.2 us
    pallas_call x1, Pallas kernels, hand_out(): pl.pallas_call(store, out_shape=(pltpu.HBM(moved.shape, moved.dtype), plt...  1.24 us

profile of v7, /device:TPU:0, one launch (start us, length us, event | category | flops | bytes accessed | tf_op | source)
XLA Modules:
  0.0 35.1 jit_solution(2197941716601171245)
XLA Ops:
  0.6 0.0 copy-start.1
  0.6 0.0 copy-start
  0.7 0.0 copy-start.2
  0.7 33.2 %shard_map.59 = (f32[12,32,1024]{2,1,0:T(8,128)S(1)}, f32[2,32,1024]{2,1,0:T(8,128)S(1)}, f32[1]{0:T(128)S(4)}) custom-call(f32[12,256,128]{2,1,0:T(8,128)} %bitcast.8, s32[32]{0:T(128)} %offs_in.1, f32[2,32,1024]{2,1,0:T(8,128)} %visc_in.1, f32[2,32,1024]{2,1,0:T(8,128)} %absorb_in.1), custom_call_target="tpu_custom_call" | custom-call | tf_op jit(solution)/shard_map/pallas_call | solution.py:830
  33.8 0.0 copy-done.1
  33.9 0.0 copy-done
  33.9 0.0 copy-done.2
  33.9 1.2 %shard_map.60 = (f32[12,32,1024]{2,1,0:T(8,128)}, f32[2,32,1024]{2,1,0:T(8,128)}) custom-call(f32[12,32,1024]{2,1,0:T(8,128)S(1)} %get-tuple-element.28.a, f32[2,32,1024]{2,1,0:T(8,128)S(1)} %get-tuple-element.29.b), custom_call_target="tpu_custom_call" | custom-call | tf_op jit(solution)/shard_map/pallas_call | solution.py:881
  (1 shorter events, 0.0 us)
Async XLA Ops:
  0.6 33.2 %copy-start.1 = (f32[2,32,1024]{2,1,0:T(8,128)S(1)}, f32[2,32,1024]{2,1,0:T(8,128)}, u32[]{:S(2)}) copy-start(f32[2,32,1024]{2,1,0:T(8,128)} %absorb_in.1) | copy-start | bytes 786436
  0.6 33.2 %copy-start = (f32[2,32,1024]{2,1,0:T(8,128)S(1)}, f32[2,32,1024]{2,1,0:T(8,128)}, u32[]{:S(2)}) copy-start(f32[2,32,1024]{2,1,0:T(8,128)} %visc_in.1) | copy-start | bytes 786436
  0.7 33.2 %copy-start.2 = (s32[32]{0:T(128)S(1)}, s32[32]{0:T(128)}, u32[]{:S(2)}) copy-start(s32[32]{0:T(128)} %offs_in.1) | copy-start | bytes 388

commit v8 on v6

--- a/solution.py
+++ b/solution.py
@@ -779,7 +779,7 @@
     scan_send()
     pending = []
     for f in order[1:-1]:
-        if f == order[2]:
+        if f == order[3]:
             last_edges = early_edges()
         pending.append((f, work(f)))
         if len(hops) < n_scan:

time: 35.3 us -> 35.3 us (level)
  no operation moved by 1% of the time
where the time goes in v8:
time: 35.3 us; the launch traced here: 35.2 us
  Pallas kernels  34.5 us (98%)
  between operations  0.7 us (2%)
    pallas_call x1, Pallas kernels, fast(): pl.pallas_call(functools.partial(fast_kernel, n_rad, n_az, cap, dust_cap)...  33.2 us
    pallas_call x1, Pallas kernels, hand_out(): pl.pallas_call(store, out_shape=(pltpu.HBM(moved.shape, moved.dtype), plt...  1.24 us

profile of v8, /device:TPU:0, one launch (start us, length us, event | category | flops | bytes accessed | tf_op | source)
XLA Modules:
  0.0 35.2 jit_solution(994435504532734756)
XLA Ops:
  0.6 0.0 copy-start.1
  0.6 0.0 copy-start
  0.7 0.0 copy-start.2
  0.7 33.2 %shard_map.59 = (f32[12,32,1024]{2,1,0:T(8,128)S(1)}, f32[2,32,1024]{2,1,0:T(8,128)S(1)}, f32[1]{0:T(128)S(4)}) custom-call(f32[12,256,128]{2,1,0:T(8,128)} %bitcast.8, s32[32]{0:T(128)} %offs_in.1, f32[2,32,1024]{2,1,0:T(8,128)} %visc_in.1, f32[2,32,1024]{2,1,0:T(8,128)} %absorb_in.1), custom_call_target="tpu_custom_call" | custom-call | tf_op jit(solution)/shard_map/pallas_call | solution.py:826
  33.9 0.0 copy-done.1
  33.9 0.0 copy-done
  33.9 0.0 copy-done.2
  34.0 1.2 %shard_map.60 = (f32[12,32,1024]{2,1,0:T(8,128)}, f32[2,32,1024]{2,1,0:T(8,128)}) custom-call(f32[12,32,1024]{2,1,0:T(8,128)S(1)} %get-tuple-element.28.a, f32[2,32,1024]{2,1,0:T(8,128)S(1)} %get-tuple-element.29.b), custom_call_target="tpu_custom_call" | custom-call | tf_op jit(solution)/shard_map/pallas_call | solution.py:877
  (1 shorter events, 0.0 us)
Async XLA Ops:
  0.6 33.3 %copy-start.1 = (f32[2,32,1024]{2,1,0:T(8,128)S(1)}, f32[2,32,1024]{2,1,0:T(8,128)}, u32[]{:S(2)}) copy-start(f32[2,32,1024]{2,1,0:T(8,128)} %absorb_in.1) | copy-start | bytes 786436
  0.6 33.3 %copy-start = (f32[2,32,1024]{2,1,0:T(8,128)S(1)}, f32[2,32,1024]{2,1,0:T(8,128)}, u32[]{:S(2)}) copy-start(f32[2,32,1024]{2,1,0:T(8,128)} %visc_in.1) | copy-start | bytes 786436
  0.7 33.3 %copy-start.2 = (s32[32]{0:T(128)S(1)}, s32[32]{0:T(128)}, u32[]{:S(2)}) copy-start(s32[32]{0:T(128)} %offs_in.1) | copy-start | bytes 388
